TPU v7x, 32 devices: a whole 2x2x4 slice. The times are simulated.
32 devices in a mesh: filt: 2 (over y), chan: 4 (over x, core), tile: 4 (over z).
Axes of the slice: x: 2, y: 2, z: 4, core: 2. Of those that a mesh axis runs over, the one named last changes fastest.
Arguments:
- saved_input: bfloat16 [256, 48, 2048], P('tile', 'filt', 'chan'), may hold values from -1.5 to 1.5
- upstream: bfloat16 [256, 48, 2048], P('tile', None, 'filt'), may hold values from -4 to 4
- kernel: bfloat16 [3, 3, 2048, 2048], P(None, None, 'chan', 'filt'), may hold values from -0.046875 to 0.046875
Outputs:
- input_grad: bfloat16 [256, 48, 2048], P('tile', 'filt', 'chan')
- kernel_grad: float32 [3, 3, 2048, 2048], P(None, None, ('chan', 'tile'), 'filt')
All inputs are finite; a program needn't handle non-finite values.
Results may differ from a plain program's by a relative error of at most 0.014.
Values may be sent and summed in bfloat16 or wider, within the bound.
No kernel may reach another device: no remote copies, remote signals or barrier semaphores. Data moves between devices by JAX's collectives and lax.ppermute only.
A program may use at most 192 MiB of HBM per device.

v0:
```python
import jax
import jax.numpy as jnp
from jax import lax
from jax.sharding import PartitionSpec as P


def padded_2(value, sides, width):
    for axis, dim in sides:
        count, length = (lax.axis_size(axis), value.shape[dim])
        up = [(i, (i + 1) % count) for i in range(count - 1)]
        down = [(j, i) for i, j in up]
        last = lax.slice_in_dim(value, length - width, length, axis=dim)
        leading = lax.slice_in_dim(value, 0, width, axis=dim)
        before = lax.ppermute(last, axis, up)
        after = lax.ppermute(leading, axis, down)
        value = jnp.concatenate([before, value, after], axis=dim)
    return value


def shifted_blocks(padded, height, breadth, direction):
    pieces = []
    for step_row in (-1, 0, 1):
        for step_col in (-1, 0, 1):
            top = 1 + direction * step_row
            left = 1 + direction * step_col
            pieces.append(padded[top : top + height, left : left + breadth])
    return jnp.concatenate(pieces, axis=2)


def per_device(saved_input, upstream, kernel):
    height, breadth, out_width = upstream.shape
    in_width = kernel.shape[2]
    active = jnp.maximum(saved_input, jnp.zeros((), jnp.bfloat16))
    gathered = lax.all_gather(active, "filt", axis=1, tiled=True)
    rimmed_grad = padded_2(upstream, (("tile", 0),), 1)
    padded_grad = jnp.pad(rimmed_grad, ((0, 0), (1, 1), (0, 0)))
    stacked_grad = shifted_blocks(padded_grad, height, breadth, -1).reshape(
        height * breadth, 9 * out_width
    )
    kernel_flat = jnp.transpose(kernel.reshape(9, in_width, out_width), (0, 2, 1)).reshape(
        9 * out_width, in_width
    )
    partial_value = jnp.dot(stacked_grad, kernel_flat, preferred_element_type=jnp.float32).reshape(
        height, breadth, in_width
    )
    summed = lax.psum_scatter(
        partial_value.astype(jnp.bfloat16), "filt", scatter_dimension=1, tiled=True
    ).astype(jnp.float32)
    masked = jnp.where(saved_input > 0, summed, jnp.zeros((), jnp.float32))
    input_grad = masked.astype(jnp.bfloat16)
    rimmed_input = padded_2(gathered, (("tile", 0),), 1)
    padded_input = jnp.pad(rimmed_input, ((0, 0), (1, 1), (0, 0)))
    stacked_input = shifted_blocks(padded_input, height, breadth, 1).reshape(
        height * breadth, 9 * in_width
    )
    kernel_part = jnp.dot(
        stacked_input.T,
        upstream.reshape(height * breadth, out_width),
        preferred_element_type=jnp.float32,
    )
    kernel_part = kernel_part.reshape(3, 3, in_width, out_width)
    kernel_grad = lax.psum_scatter(
        kernel_part.astype(jnp.bfloat16), "tile", scatter_dimension=2, tiled=True
    ).astype(jnp.float32)
    return (input_grad, kernel_grad)


def solution(mesh):
    placed = (P("tile", "filt", "chan"), P("tile", None, "filt"), P(None, None, "chan", "filt"))
    return jax.shard_map(
        per_device,
        mesh=mesh,
        in_specs=placed,
        out_specs=(P("tile", "filt", "chan"), P(None, None, ("chan", "tile"), "filt")),
        check_vma=False,
    )
```

profile of v0, /device:TPU:9, one launch (start us, length us, event | category | flops | bytes accessed | tf_op | source)
XLA Modules:
  0.0 385.4 jit_solution(7531991701622401703)
XLA Ops:
  7.2 1.0 fusion.16
  8.2 1.9 collective-permute-start.1
  10.1 3.4 collective-permute-start
  13.5 2.7 broadcast_maximum_fusion
  16.2 13.0 %copy.7 = bf16[9,1024,512]{2,1,0:T(8,128)(2,1)} copy(bf16[9,1024,512]{1,2,0:T(8,128)(2,1)} %bitcast.34) | data formatting | bytes 18874368 | tf_op jit(solution)/shard_map/transpose | solution.py:40
  29.2 5.8 %fusion.5 = bf16[66,50,1024]{2,1,0:T(8,128)(2,1)S(1)} fusion(bf16[1,48,1024]{2,1,0:T(8,128)(2,1)S(1)} %collective-permute-done.1, bf16[64,48,1024]{2,1,0:T(8,128)(2,1)} %param.4, bf16[1,48,1024]{2,1,0:T(8,128)(2,1)S(1)} %collective-permute-done), kind=kLoop, calls=%fused_computation.9 | loop fusion | flops 40550400 | bytes 13246464 | tf_op jit(solution)/shard_map/concatenate | solution.py:16
  35.0 5.4 %slice_dynamic-update-slice_fusion.5 = bf16[64,48,9216]{2,1,0:T(8,128)(2,1)} fusion(bf16[66,50,1024]{2,1,0:T(8,128)(2,1)S(1)} %fusion.5), kind=kLoop, calls=%fused_computation.21 | loop fusion | bytes 12582912
  40.3 3.6 fusion.8
  43.9 3.5 slice_dynamic-update-slice_fusion.4
  47.5 6.8 %slice_dynamic-update-slice_fusion.3 = bf16[64,48,9216]{2,1,0:T(8,128)(2,1)} fusion(bf16[64,48,9216]{2,1,0:T(8,128)(2,1)} %slice_dynamic-update-slice_fusion.4, bf16[66,50,1024]{2,1,0:T(8,128)(2,1)S(1)} %fusion.5), kind=kLoop, calls=%fused_computation.17 | loop fusion | bytes 12582912
  54.2 3.6 constant_dynamic-update-slice_fusion
  57.9 3.4 slice_dynamic-update-slice_fusion.2
  61.3 7.1 %slice_dynamic-update-slice_fusion.1 = bf16[64,48,9216]{2,1,0:T(8,128)(2,1)} fusion(bf16[64,48,9216]{2,1,0:T(8,128)(2,1)} %slice_dynamic-update-slice_fusion.2, bf16[66,50,1024]{2,1,0:T(8,128)(2,1)S(1)} %fusion.5), kind=kLoop, calls=%fused_computation.15 | loop fusion | bytes 12582912
  68.3 3.5 fusion.7
  71.8 3.4 slice_dynamic-update-slice_fusion
  75.3 0.8 fusion.17
  76.1 1.9 collective-permute-start.3
  78.0 3.4 collective-permute-start.2
  81.4 36.7 %fusion.18 = bf16[6,8,64,512]{3,1,0,2:T(8,128)(2,1)S(1)} fusion(bf16[64,48,9216]{2,1,0:T(8,128)(2,1)} %slice_dynamic-update-slice_fusion, bf16[9216,512,1]{1,0,2:T(8,128)(2,1)} %bitcast.35), kind=kOutput, calls=%fused_computation.44 | convolution fusion | flops 28992602112 | bytes 69206016 | tf_op jit(solution)/shard_map/dot_general | solution.py:43
  118.1 2.0 copy.12
  120.2 1.0 copy-done
  121.1 1.9 fusion.13
  123.7 1.6 slice_dynamic-update-slice_fusion.10
  126.1 1.6 slice_dynamic-update-slice_fusion.8
  128.4 1.6 slice_dynamic-update-slice_fusion.6
  130.0 9.5 %copy-done.1 = bf16[64,48,4608]{2,1,0:T(8,128)(2,1)} copy-done((bf16[64,48,4608]{2,1,0:T(8,128)(2,1)}, bf16[64,48,4608]{2,1,0:T(8,128)(2,1)S(1)}, u32[]{:S(2)}) %copy-start.1) | copy-done | bytes 28311576
  139.5 36.8 %copy.8 = bf16[3072,4608]{0,1:T(8,128)(2,1)} copy(bf16[3072,4608]{1,0:T(8,128)(2,1)} %bitcast.31) | data formatting | bytes 56623104 | tf_op jit(solution)/shard_map/reshape | solution.py:53
  176.3 35.6 %convolution_convert_fusion = bf16[3,3,512,1024]{3,2,1,0:T(8,128)(2,1)} fusion(bf16[3,3,512,3072]{3,2,1,0:T(8,128)(2,1)} %bitcast.32, bf16[3072,1024,1,1]{1,0,3,2:T(8,128)(2,1)} %bitcast.28), kind=kOutput, calls=%fused_computation.11 | convolution fusion | flops 28995747840 | bytes 44040192 | tf_op jit(solution)/shard_map/dot_general | solution.py:56
  212.0 2.0 copy.13
  214.0 2.4 select_convert_fusion
  216.4 158.1 %reduce-scatter.5.cloned.1.call-done = bf16[3,3,128,1024]{3,2,1,0:T(8,128)(2,1)} async-done(((bf16[3,3,512,1024]{3,2,1,0:T(8,128)(2,1)}), bf16[3,3,128,1024]{3,2,1,0:T(8,128)(2,1)}) %reduce-scatter.5.cloned.1.call-update) | async-done | bytes 2359312 | tf_op jit(solution)/shard_map/reduce_scatter | solution.py:62
  374.5 4.4 %convert_element_type.23 = f32[3,3,128,1024]{3,2,1,0:T(8,128)} convert(bf16[3,3,128,1024]{3,2,1,0:T(8,128)(2,1)} %reduce-scatter.5.cloned.1.call-done) | non-fusion elementwise | flops 1179648 | bytes 7077888 | tf_op jit(solution)/shard_map/convert_element_type | solution.py:64
  (27 shorter events, 2.2 us)
Async XLA Ops:
  7.2 68.1 %all-gather.2.cloned.1.call-start = ((), (), s32[]{:S(2)}) async-start(), calls=%async_computation.2 | async-start | bytes 4718592 | tf_op jit(solution)/shard_map/all_gather | solution.py:34
  8.2 21.0 %collective-permute-start.1 = (bf16[1,48,1024]{2,1,0:T(8,128)(2,1)S(1)}, bf16[1,48,1024]{2,1,0:T(8,128)(2,1)S(1)}, u32[]{:S(2)}, u32[]{:S(2)}) collective-permute-start(bf16[1,48,1024]{2,1,0:T(8,128)(2,1)S(1)} %get-tuple-element.3), channel_id=1, source_target_pairs={{1,0},{2,1},{3,2},{5,4},{6,5},{7,6},{9,8},{10,9},{11,10},{13,12},{... | collective-permute-start | bytes 294920 | tf_op jit(solution)/shard_map/ppermute | solution.py:15
  10.1 19.1 %collective-permute-start = (bf16[1,48,1024]{2,1,0:T(8,128)(2,1)S(1)}, bf16[1,48,1024]{2,1,0:T(8,128)(2,1)S(1)}, u32[]{:S(2)}, u32[]{:S(2)}) collective-permute-start(bf16[1,48,1024]{2,1,0:T(8,128)(2,1)S(1)} %get-tuple-element.2), channel_id=1, source_target_pairs={{0,1},{1,2},{2,3},{4,5},{5,6},{6,7},{8,9},{9,10},{10,11},{12,13},{... | collective-permute-start | bytes 294920 | tf_op jit(solution)/shard_map/ppermute | solution.py:14
  16.1 195.8 %reduce-scatter.7.cloned.1.call-start = ((), (), s32[]{:S(2)}) async-start(), calls=%async_computation.4 | async-start | bytes 4718592
  16.2 24.1 %slice-start = ((s8[6291456]{0:T(1024)(128)(4,1)}), s8[2097152]{0:T(1024)(128)(4,1)S(1)}, s32[]{:S(2)}) async-start(s8[6291456]{0:T(1024)(128)(4,1)} %bitcast.29), calls=%async_computation.5 | async-start | bytes 4194304
  29.2 11.2 %slice-start.1 = ((s8[6291456]{0:T(1024)(128)(4,1)}), s8[4194304]{0:T(1024)(128)(4,1)S(1)}, s32[]{:S(2)}) async-start(s8[6291456]{0:T(1024)(128)(4,1)} %bitcast.29), calls=%async_computation.6 | async-start | bytes 8388608
  76.1 44.0 %collective-permute-start.3 = (bf16[1,48,512]{2,1,0:T(8,128)(2,1)S(1)}, bf16[1,48,512]{2,1,0:T(8,128)(2,1)S(1)}, u32[]{:S(2)}, u32[]{:S(2)}) collective-permute-start(bf16[1,48,512]{2,1,0:T(8,128)(2,1)S(1)} %get-tuple-element.5), channel_id=1, source_target_pairs={{1,0},{2,1},{3,2},{5,4},{6,5},{7,6},{9,8},{10,9},{11,10},{13,12},{... | collective-permute-start | bytes 147464 | tf_op jit(solution)/shard_map/ppermute | solution.py:15
  78.0 42.1 %collective-permute-start.2 = (bf16[1,48,512]{2,1,0:T(8,128)(2,1)S(1)}, bf16[1,48,512]{2,1,0:T(8,128)(2,1)S(1)}, u32[]{:S(2)}, u32[]{:S(2)}) collective-permute-start(bf16[1,48,512]{2,1,0:T(8,128)(2,1)S(1)} %get-tuple-element.4), channel_id=1, source_target_pairs={{0,1},{1,2},{2,3},{4,5},{5,6},{6,7},{8,9},{9,10},{10,11},{12,13},{... | collective-permute-start | bytes 147464 | tf_op jit(solution)/shard_map/ppermute | solution.py:14
  118.1 3.0 copy-start
  120.1 254.4 %reduce-scatter.5.cloned.1.call-start = ((), (), s32[]{:S(2)}) async-start(), calls=%async_computation.3 | async-start | bytes 11796480 | tf_op jit(solution)/shard_map/reduce_scatter | solution.py:62
  130.0 9.5 %copy-start.1 = (bf16[64,48,4608]{2,1,0:T(8,128)(2,1)}, bf16[64,48,4608]{2,1,0:T(8,128)(2,1)S(1)}, u32[]{:S(2)}) copy-start(bf16[64,48,4608]{2,1,0:T(8,128)(2,1)S(1)} %slice_dynamic-update-slice_fusion.6) | copy-start | bytes 84934656
  211.9 2.1 copy-start.2
Sparse Core Ops, SparseCore 0:
  16.3 45.6 all-gather.1
  120.2 44.5 reduce-scatter.6
  212.1 162.3 reduce-scatter.4
where the time goes:
time: 389 us; the launch traced here: 385 us
  waiting for transfers between devices  158 us (41%)
  local copies, waits for them, and re-layouts  106 us (27%)
  matrix products  72.3 us (19%)
  other arithmetic  24.7 us (6%)
  between operations  13.9 us (4%)
  starting transfers between devices  10.7 us (3%)
    reduce_scatter x1, waiting for transfers between devices, per_device(): lax.psum_scatter(kernel_part.astype(jnp.bfloat16), 'tile', scatter_dimens...  158 us
    unnamed x24, local copies, waits for them, and re-layouts  49 us
    reshape x1, local copies, waits for them, and re-layouts, per_device(): shifted_blocks(padded_input, height, breadth, 1)  36.8 us
    dot_general x1, matrix products, per_device(): jnp.dot(stacked_grad, kernel_flat, preferred_element_type=jnp.float32)  36.7 us
    dot_general x1, matrix products, per_device(): jnp.dot(stacked_input.T, upstream.reshape(height * breadth, out_width), p...  35.6 us
    transpose x1, local copies, waits for them, and re-layouts, per_device(): jnp.transpose(kernel.reshape(9, in_width, out_width), (0, 2, 1))  13 us
  transfers between devices with their start and end apart: 7, of which 1 were waited for; matrix products, arithmetic and copies ran while one was open for 48% of the time, Pallas kernels for 0%

commit v1 on v0

v1 whole, which is shorter than its diff:
```python
import jax
import jax.numpy as jnp
from jax import lax
from jax.experimental import pallas as pl
from jax.experimental.pallas import tpu as pltpu
from jax.sharding import PartitionSpec as P

LANES = 128
VMEM = 56 << 20


def largest(total, most):
    return max(n for n in range(1, most + 1) if total % n == 0)


def cost(flops, moved):
    return pl.CostEstimate(flops=flops, bytes_accessed=moved, transcendentals=0)


def params():
    return pltpu.CompilerParams(vmem_limit_bytes=VMEM)


def swap(value, axis, bit):
    count = lax.axis_size(axis)
    return lax.ppermute(value, axis, [(i, i ^ bit) for i in range(count)])


def shifted_active(parts, side):
    height, part, depth = parts[0].shape
    breadth = part * len(parts)
    rows = largest(height, 16)
    span = rows * breadth

    def body(side_ref, *refs):
        *part_refs, out_ref = refs
        read = [ref[...].astype(jnp.float32) for ref in part_refs]
        if len(read) == 2:
            whole = jnp.where(
                side_ref[0] == 0, jnp.concatenate(read, 1), jnp.concatenate(read[::-1], 1)
            )
        else:
            whole = read[0]
        active = jnp.maximum(whole, 0.0).reshape(span, depth).T
        column = lax.broadcasted_iota(jnp.int32, active.shape, 1) % breadth
        before = jnp.where(column == 0, 0.0, pltpu.roll(active, 1, 1))
        after = jnp.where(column == breadth - 1, 0.0, pltpu.roll(active, span - 1, 1))
        out_ref[0] = before.astype(jnp.bfloat16)
        out_ref[1] = active.astype(jnp.bfloat16)
        out_ref[2] = after.astype(jnp.bfloat16)

    return pl.pallas_call(
        body,
        grid_spec=pltpu.PrefetchScalarGridSpec(
            num_scalar_prefetch=1,
            grid=(height // rows,),
            in_specs=[pl.BlockSpec((rows, part, depth), lambda i, s: (i, 0, 0))] * len(parts),
            out_specs=pl.BlockSpec((3, depth, span), lambda i, s: (0, 0, i)),
        ),
        out_shape=jax.ShapeDtypeStruct((3, depth, height * breadth), jnp.bfloat16),
        compiler_params=params(),
        cost_estimate=cost(0, 8 * height * breadth * depth),
        name="shifted_active",
    )(side, *parts)


def kernel_sums(blocks, own_active, pair_active, own_grad, pair_grads, dtype, pair_place=0):
    depth = own_active.shape[1]
    height, breadth, width = pair_grads[0].shape
    height, count = height - 2, len(pair_grads)
    rows = largest(height, 16)
    steps, span, total = height // rows, rows * breadth, width * count

    def body(blocks_ref, own_a, pair_a, *refs):
        own_g, pair_g = refs[:count], refs[count : 2 * count]
        out_ref, sums = refs[2 * count :]
        step = pl.program_id(0)

        def add(active_ref, grad_refs, first_row, fresh):
            active = active_ref[...].reshape(3 * depth, span)
            for r in range(3):
                grads = [
                    ref[pl.ds(first_row + 2 - r, rows)].reshape(span, width) for ref in grad_refs
                ]
                grad = grads[0] if count == 1 else jnp.concatenate(grads, 1)
                product = jnp.dot(active, grad, preferred_element_type=jnp.float32)
                if fresh:
                    sums[r] = product
                else:
                    sums[r] += product

        @pl.when(step == 0)
        def _():
            add(own_a, own_g, 0, True)

        @pl.when((step > 0) & (step < steps))
        def _():
            add(own_a, own_g, step * rows, False)

        @pl.when(step >= steps)
        def _():
            add(pair_a, pair_g, (step - steps) * rows, False)

        @pl.when(step == 2 * steps - 1)
        def _():
            out_ref[...] = sums[...].astype(dtype)

    def own_block(k):
        return pl.BlockSpec((height + 2, breadth, width), lambda i, b: (0, 0, b[k]))

    moved = 2 * (6 * depth + 2 * total) * height * breadth + 9 * depth * total * 4
    return pl.pallas_call(
        body,
        grid_spec=pltpu.PrefetchScalarGridSpec(
            num_scalar_prefetch=1,
            grid=(2 * steps,),
            in_specs=[
                pl.BlockSpec((3, depth, span), lambda i, b: (0, 0, jnp.minimum(i, steps - 1))),
                pl.BlockSpec(
                    (3, depth, span),
                    lambda i, b: (0, 0, jnp.maximum(i - steps, 0) + pair_place * steps),
                ),
                *[own_block(k) for k in range(count)],
                *[pl.BlockSpec((height + 2, breadth, width), lambda i, b: (0, 0, 0))] * count,
            ],
            out_specs=pl.BlockSpec((3, 3 * depth, total), lambda i, b: (0, 0, 0)),
            scratch_shapes=[pltpu.VMEM((3, 3 * depth, total), jnp.float32)],
        ),
        out_shape=jax.ShapeDtypeStruct((3, 3 * depth, total), dtype),
        compiler_params=params(),
        cost_estimate=cost(4 * 9 * depth * total * height * breadth, moved),
        name="kernel_sums",
    )(blocks, own_active, pair_active, *[own_grad] * count, *pair_grads)


def add_block(blocks, near, arrived, out, width, full):
    taps, depth, total = near.shape

    def body(blocks_ref, near_ref, arrived_ref, *refs):
        refs[-1][...] = near_ref[...] + arrived_ref[...].astype(jnp.float32)

    block = (taps, depth, width)
    return pl.pallas_call(
        body,
        grid_spec=pltpu.PrefetchScalarGridSpec(
            num_scalar_prefetch=1,
            grid=(total // width,),
            in_specs=[pl.BlockSpec(block, lambda i, b: (0, 0, i))] * 2
            + [pl.BlockSpec(memory_space=pl.ANY)] * (out is not None),
            out_specs=pl.BlockSpec(block, lambda i, b: (0, 0, b[i])),
        ),
        out_shape=jax.ShapeDtypeStruct((taps, depth, full), jnp.float32),
        input_output_aliases={} if out is None else {3: 0},
        compiler_params=params(),
        cost_estimate=cost(taps * depth * total, 10 * taps * depth * total),
        name="add_block",
    )(blocks, near, arrived, *([] if out is None else [out]))


def block_grad(grad, weights, start, count):
    height, breadth, filters = grad.shape
    depth = weights.shape[1] // 3
    rows = largest(count, 16)
    span = rows * breadth
    lane = min(depth, LANES)

    def body(grad_ref, weights_ref, out_ref, sums):
        first = start + pl.program_id(0) * rows
        for r in range(3):
            moved = grad_ref[pl.ds(first + 2 - r, rows)].reshape(span, filters)
            for s in range(3):
                product = lax.dot_general(
                    moved,
                    weights_ref[r, s * depth : (s + 1) * depth, :],
                    (((1,), (1,)), ((), ())),
                    preferred_element_type=jnp.float32,
                )
                if r == 0:
                    sums[s] = product
                else:
                    sums[s] += product
        column = lax.broadcasted_iota(jnp.int32, (span, lane), 0) % breadth
        for low in range(0, depth, lane):
            before = pltpu.roll(sums[2, :, low : low + lane], 1, 0)
            after = pltpu.roll(sums[0, :, low : low + lane], span - 1, 0)
            value = (
                sums[1, :, low : low + lane]
                + jnp.where(column == 0, 0.0, before)
                + jnp.where(column == breadth - 1, 0.0, after)
            )
            out_ref[:, :, low : low + lane] = value.astype(jnp.bfloat16).reshape(
                rows, breadth, lane
            )

    return pl.pallas_call(
        body,
        grid=(count // rows,),
        in_specs=[
            pl.BlockSpec(
                (height, breadth, filters), lambda i: (0, 0, 0), pipeline_mode=pl.Buffered(1)
            ),
            pl.BlockSpec(weights.shape, lambda i: (0, 0, 0), pipeline_mode=pl.Buffered(1)),
        ],
        out_specs=pl.BlockSpec((rows, breadth, depth), lambda i: (i, 0, 0)),
        scratch_shapes=[pltpu.VMEM((3, span, depth), jnp.float32)],
        out_shape=jax.ShapeDtypeStruct((count, breadth, depth), jnp.bfloat16),
        compiler_params=params(),
        cost_estimate=cost(
            18 * count * breadth * depth * filters, 2 * (grad.size + weights.size)
        ),
        name="block_grad",
    )(grad, weights)


def per_device(saved_input, upstream, kernel):
    height, breadth, filters = upstream.shape
    part = saved_input.shape[1]
    channels = kernel.shape[2]
    tiles, chans, filts = (lax.axis_size(a) for a in ("tile", "chan", "filt"))
    tile, chan, filt = (lax.axis_index(a) for a in ("tile", "chan", "filt"))
    depth = channels // tiles
    side = jnp.reshape(filt, (1,)).astype(jnp.int32)

    up = [(i, i + 1) for i in range(tiles - 1)]
    before = lax.ppermute(upstream[height - 1 :], "tile", up)
    after = lax.ppermute(upstream[:1], "tile", [(j, i) for i, j in up])

    def chunk(bits):
        return lax.dynamic_slice_in_dim(saved_input, (tile ^ bits) * depth, depth, axis=2)

    def columns(value):
        if filts == 2:
            return [value, swap(value, "filt", 1)]
        return [lax.all_gather(value, "filt", axis=1, tiled=True)]

    pair_far = swap(chunk(2), "tile", 1)
    own_far_active = shifted_active(columns(chunk(3)), side)

    def border(low, width):
        return jnp.concatenate(
            [lax.dynamic_slice_in_dim(v, low, width, axis=2) for v in (before, upstream, after)],
            axis=0,
        )

    if chans == 4 and filters % (chans * LANES) == 0:
        share = filters // chans
        width = LANES
        groups = []
        for low in range(0, share, width):
            mine = swap(border(chan * share + low, width), "tile", 1)
            across = swap(mine, "chan", 2)
            groups.append(
                [
                    (0, low, mine),
                    (1, low, swap(mine, "chan", 1)),
                    (2, low, across),
                    (3, low, swap(across, "chan", 1)),
                ]
            )
        groups = [g[:2] for g in groups] + [g[2:] for g in groups]
        pieces = [
            (
                jnp.stack([((chan ^ k) * share + low) // width for k, low, _ in g]).astype(
                    jnp.int32
                ),
                [v for _, _, v in g],
            )
            for g in groups
        ]
    else:
        width = filters
        pieces = [(jnp.zeros((1,), jnp.int32), [swap(border(0, filters), "tile", 1)])]

    pair_far_active = shifted_active(columns(pair_far), side)
    pair_near = swap(chunk(1), "tile", 1)
    near_active = shifted_active(
        columns(jnp.concatenate([chunk(0), pair_near], axis=0)), side
    )

    rimmed = jnp.concatenate([before, upstream, after], axis=0)
    weights = kernel.reshape(3, 3 * channels, filters)

    arrived = []
    for blocks, grads in pieces:
        far = kernel_sums(blocks, own_far_active, pair_far_active, rimmed, grads, jnp.bfloat16)
        arrived.append(swap(far, "tile", 3))

    halves = 2 if height % 2 == 0 else 1
    count = height // halves
    input_grads = []
    for half in range(halves):
        partial = block_grad(rimmed, weights, half * count, count)
        if filts == 2:
            mine = lax.dynamic_slice_in_dim(partial, filt * part, part, axis=1)
            other = lax.dynamic_slice_in_dim(partial, (1 - filt) * part, part, axis=1)
            other = swap(other, "filt", 1)
            summed = mine.astype(jnp.float32) + other.astype(jnp.float32)
        else:
            summed = lax.psum_scatter(
                partial, "filt", scatter_dimension=1, tiled=True
            ).astype(jnp.float32)
        saved = saved_input[half * count : (half + 1) * count]
        input_grads.append(
            jnp.where(saved > 0, summed, jnp.zeros((), jnp.float32)).astype(jnp.bfloat16)
        )
    input_grad = jnp.concatenate(input_grads, axis=0)

    out = None
    for (blocks, grads), result in zip(pieces, arrived):
        near = kernel_sums(
            blocks, near_active, near_active, rimmed, grads, jnp.float32, pair_place=1
        )
        out = add_block(blocks, near, result, out, width, filters)
    return input_grad, out.reshape(3, 3, depth, filters)


def solution(mesh):
    placed = (P("tile", "filt", "chan"), P("tile", None, "filt"), P(None, None, "chan", "filt"))
    return jax.shard_map(
        per_device,
        mesh=mesh,
        in_specs=placed,
        out_specs=(P("tile", "filt", "chan"), P(None, None, ("chan", "tile"), "filt")),
        check_vma=False,
    )
```

time: 389 us -> 271 us (0.70)
  Pallas kernels: 0 us -> 156 us
  waiting for transfers between devices: 158 us -> 60.4 us
  local copies, waits for them, and re-layouts: 106 us -> 22.2 us
  matrix products: 72.3 us -> 0 us
  other arithmetic: 24.7 us -> 8.69 us
  between operations: 13.9 us -> 0.84 us
  starting transfers between devices: 10.7 us -> 20.6 us
    reduce_scatter x1 -> x0, waiting for transfers between devices: 158 us -> none  [per_device(): lax.psum_scatter(kernel_part.astype(jnp.bfloat16), 'tile', scatter_dimens...]
    pallas_call x0 -> x17, Pallas kernels: none -> 156 us  [the longest x8 85.1 us: kernel_sums(): pl.pallas_call(body, grid_spec=pltpu.PrefetchScalarGridSpec(num_scalar_pr...]
    dot_general x2 -> x0, matrix products: 72.3 us -> none  [the longest x1 36.7 us: per_device(): jnp.dot(stacked_grad, kernel_flat, preferred_element_type=jnp.float32)]
    ppermute x4 -> x21, waiting for transfers between devices: 0.01 us -> 60.4 us  [the longest x19 60.4 us: swap(): return lax.ppermute(value, axis, [(i, i ^ bit) for i in range(count)])]
    reshape x1 -> x0, local copies, waits for them, and re-layouts: 36.8 us -> none  [per_device(): shifted_blocks(padded_input, height, breadth, 1)]
    unnamed x24 -> x40, local copies, waits for them, and re-layouts: 49 us -> 14.4 us
    transpose x1 -> x0, local copies, waits for them, and re-layouts: 13 us -> none  [per_device(): jnp.transpose(kernel.reshape(9, in_width, out_width), (0, 2, 1))]
    ppermute x4 -> x21, starting transfers between devices: 10.6 us -> 20.6 us  [the longest x19 15.4 us: swap(): return lax.ppermute(value, axis, [(i, i ^ bit) for i in range(count)])]
  transfers between devices with their start and end apart: 7 -> 21, of which waited for: 1 -> 3; matrix products, arithmetic and copies ran while one was open for 48% -> 7% of each run, Pallas kernels for 0% -> 57%
where the time goes in v1:
time: 271 us; the launch traced here: 269 us
  Pallas kernels  156 us (58%)
  waiting for transfers between devices  60.4 us (22%)
  local copies, waits for them, and re-layouts  22.2 us (8%)
  starting transfers between devices  20.6 us (8%)
  other arithmetic  8.69 us (3%)
    pallas_call x8, Pallas kernels, kernel_sums(): pl.pallas_call(body, grid_spec=pltpu.PrefetchScalarGridSpec(num_scalar_pr...  85.1 us
    ppermute x19, waiting for transfers between devices, swap(): return lax.ppermute(value, axis, [(i, i ^ bit) for i in range(count)])  60.4 us
    pallas_call x2, Pallas kernels, block_grad(): pl.pallas_call(body, grid=(count // rows,), in_specs=[pl.BlockSpec((heigh...  43.8 us
    pallas_call x3, Pallas kernels, shifted_active(): pl.pallas_call(body, grid_spec=pltpu.PrefetchScalarGridSpec(num_scalar_pr...  15.7 us
    ppermute x19, starting transfers between devices, swap(): return lax.ppermute(value, axis, [(i, i ^ bit) for i in range(count)])  15.4 us
    unnamed x40, local copies, waits for them, and re-layouts  14.4 us
    pallas_call x4, Pallas kernels, add_block(): pl.pallas_call(body, grid_spec=pltpu.PrefetchScalarGridSpec(num_scalar_pr...  11.8 us
  transfers between devices with their start and end apart: 21, of which 3 were waited for; matrix products, arithmetic and copies ran while one was open for 7% of the time, Pallas kernels for 57%

profile of v1, /device:TPU:9, one launch (start us, length us, event | category | flops | bytes accessed | tf_op | source)
XLA Modules:
  0.0 269.0 jit_solution(484824803590745478)
XLA Ops:
  0.6 1.6 fusion
  2.2 3.2 %collective-permute-start = (bf16[1,48,1024]{2,1,0:T(8,128)(2,1)S(1)}, bf16[1,48,1024]{2,1,0:T(8,128)(2,1)S(1)}, u32[]{:S(2)}, u32[]{:S(2)}) collective-permute-start(bf16[1,48,1024]{2,1,0:T(8,128)(2,1)S(1)} %get-tuple-element.5), channel_id=1, source_target_pairs={{0,1},{1,2},{2,3},{4,5},{5,6},{6,7},{8,9},{9,10},{10,11},{12,13},{... | collective-permute-start | bytes 294920 | tf_op jit(solution)/shard_map/ppermute | solution.py:225
  5.4 2.1 collective-permute-start.1
  7.5 2.7 constant_dynamic-slice_fusion.3
  11.5 1.5 collective-permute-start.10
  12.9 1.5 constant_dynamic-slice_fusion.1
  14.4 4.1 %constant_dynamic-update-slice_fusion.1 = bf16[66,48,1024]{2,1,0:T(8,128)(2,1)S(1)} fusion(bf16[66,48,1024]{2,1,0:T(8,128)(2,1)S(1)} %constant_dynamic-update-slice_fusion.2, bf16[64,48,1024]{2,1,0:T(8,128)(2,1)} %param.4), kind=kLoop, calls=%fused_computation.7 | loop fusion | bytes 12582912
  18.6 2.7 %copy-done = bf16[66,48,1024]{2,1,0:T(8,128)(2,1)} copy-done((bf16[66,48,1024]{2,1,0:T(8,128)(2,1)}, bf16[66,48,1024]{2,1,0:T(8,128)(2,1)S(1)}, u32[]{:S(2)}) %copy-start) | copy-done | bytes 6488088
  21.3 21.9 %block_grad.2 = bf16[32,48,512]{2,1,0:T(8,128)(2,1)} custom-call(bf16[66,48,1024]{2,1,0:T(8,128)(2,1)} %copy-done, bf16[3,1536,1024]{2,1,0:T(8,128)(2,1)} %bitcast.12), custom_call_target="tpu_custom_call" | custom-call | flops 14495514624 | bytes 15925248 | tf_op jit(solution)/shard_map/block_grad/pallas_call | solution.py:195
  43.2 21.9 %block_grad.3 = bf16[32,48,512]{2,1,0:T(8,128)(2,1)} custom-call(bf16[66,48,1024]{2,1,0:T(8,128)(2,1)} %copy-done, bf16[3,1536,1024]{2,1,0:T(8,128)(2,1)} %bitcast.13), custom_call_target="tpu_custom_call" | custom-call | flops 14495514624 | bytes 15925248 | tf_op jit(solution)/shard_map/block_grad/pallas_call | solution.py:195
  73.2 37.0 %collective-permute-done.11.refs_1_ = bf16[64,24,128]{2,1,0:T(8,128)(2,1)S(1)} collective-permute-done((bf16[64,24,128]{2,1,0:T(8,128)(2,1)}, bf16[64,24,128]{2,1,0:T(8,128)(2,1)S(1)}, u32[]{:S(2)}, u32[]{:S(2)}) %collective-permute-start.11) | collective-permute-done | bytes 393248 | tf_op jit(solution)/shard_map/ppermute | solution.py:26
  110.5 3.3 %collective-permute-start.17 = (bf16[66,48,128]{2,1,0:T(8,128)(2,1)S(1)}, bf16[66,48,128]{2,1,0:T(8,128)(2,1)S(1)}, u32[]{:S(2)}, u32[]{:S(2)}) collective-permute-start(bf16[66,48,128]{2,1,0:T(8,128)(2,1)S(1)} %collective-permute-done.6.refs_2_), channel_id=1, source_target_pairs={{0,4},{4,0},{8,12},{12,8},{1,5},{5,1},{9,13},{13,9},{2,6},{6,2},{1... | collective-permute-start | bytes 2433032 | tf_op jit(solution)/shard_map/ppermute | solution.py:26
  115.7 4.2 %shifted_active.4.own_a = bf16[3,128,3072]{2,1,0:T(8,128)(2,1)} custom-call(s32[1]{0:T(128)} %bitcast.3.side_ref, bf16[64,24,128]{2,1,0:T(8,128)(2,1)} %get-tuple-element.9.refs_0_, bf16[64,24,128]{2,1,0:T(8,128)(2,1)} %collective-permute-done.9.refs_1_), custom_call_target="tpu_custom_call" | custom-call | bytes 3145728 | tf_op jit(solution)/shard_map/shifted_active/pallas_call | solution.py:52
  119.9 4.3 %shifted_active.5.pair_a = bf16[3,128,3072]{2,1,0:T(8,128)(2,1)} custom-call(s32[1]{0:T(128)} %bitcast.3.side_ref, bf16[64,24,128]{2,1,0:T(8,128)(2,1)} %collective-permute-done.10.refs_0_, bf16[64,24,128]{2,1,0:T(8,128)(2,1)} %copy-done.18), custom_call_target="tpu_custom_call" | custom-call | bytes 3145728 | tf_op jit(solution)/shard_map/shifted_active/pallas_call | solution.py:52
  124.2 1.3 collective-permute-start.7
  125.9 2.7 select_convert_fusion.1
  130.2 7.2 %shifted_active.3.own_a.pair_a = bf16[3,128,6144]{2,1,0:T(8,128)(2,1)} custom-call(s32[1]{0:T(128)} %bitcast.3.side_ref, bf16[128,24,128]{2,1,0:T(8,128)(2,1)} %copy-done.10, bf16[128,24,128]{2,1,0:T(8,128)(2,1)} %collective-permute-done.5.refs_1_), custom_call_target="tpu_custom_call" | custom-call | bytes 6291456 | tf_op jit(solution)/shard_map/shifted_active/pallas_call | solution.py:52
  138.2 10.5 %kernel_sums.13 = bf16[3,384,256]{2,1,0:T(8,128)(2,1)} custom-call(s32[2]{0:T(128)} %pad_add_fusion.2.blocks_ref, bf16[3,128,3072]{2,1,0:T(8,128)(2,1)} %shifted_active.4.own_a, bf16[3,128,3072]{2,1,0:T(8,128)(2,1)} %shifted_active.5.pair_a, bf16[66,48,1024]{2,1,0:T(8,128)(2,1)} %copy-done, bf16[66,48,1024]{2,1,0:T(8,128)(2,1)} %copy-done, ...), custom_call_target="tpu_custom_call" | custom-call | flops 3623878656 | bytes 9043968 | tf_op jit(solution)/shard_map/kernel_sums/pallas_call | solution.py:112
  148.7 2.0 collective-permute-start.18
  152.5 10.5 %kernel_sums.15 = bf16[3,384,256]{2,1,0:T(8,128)(2,1)} custom-call(s32[2]{0:T(128)} %pad_add_fusion.3.blocks_ref, bf16[3,128,3072]{2,1,0:T(8,128)(2,1)} %shifted_active.4.own_a, bf16[3,128,3072]{2,1,0:T(8,128)(2,1)} %shifted_active.5.pair_a, bf16[66,48,1024]{2,1,0:T(8,128)(2,1)} %copy-done, bf16[66,48,1024]{2,1,0:T(8,128)(2,1)} %copy-done, ...), custom_call_target="tpu_custom_call" | custom-call | flops 3623878656 | bytes 9043968 | tf_op jit(solution)/shard_map/kernel_sums/pallas_call | solution.py:112
  163.3 10.7 %kernel_sums.12.near_ref = f32[3,384,256]{2,1,0:T(8,128)} custom-call(s32[2]{0:T(128)} %pad_add_fusion.2.blocks_ref, bf16[3,128,6144]{2,1,0:T(8,128)(2,1)} %shifted_active.3.own_a.pair_a, bf16[3,128,6144]{2,1,0:T(8,128)(2,1)} %shifted_active.3.own_a.pair_a, bf16[66,48,1024]{2,1,0:T(8,128)(2,1)} %copy-done, bf16[66,48,1024]{2,1,0:T(8,128)(2,1)} %copy-done, ...), custom_call_target="tpu_custom_call" | custom-call | flops 3623878656 | bytes 9043968 | tf_op jit(solution)/shard_map/kernel_sums/pallas_call | solution.py:112
  174.0 10.7 %kernel_sums.14.near_ref = f32[3,384,256]{2,1,0:T(8,128)} custom-call(s32[2]{0:T(128)} %pad_add_fusion.3.blocks_ref, bf16[3,128,6144]{2,1,0:T(8,128)(2,1)} %shifted_active.3.own_a.pair_a, bf16[3,128,6144]{2,1,0:T(8,128)(2,1)} %shifted_active.3.own_a.pair_a, bf16[66,48,1024]{2,1,0:T(8,128)(2,1)} %copy-done, bf16[66,48,1024]{2,1,0:T(8,128)(2,1)} %copy-done, ...), custom_call_target="tpu_custom_call" | custom-call | flops 3623878656 | bytes 9043968 | tf_op jit(solution)/shard_map/kernel_sums/pallas_call | solution.py:112
  184.7 17.4 %collective-permute-done.20.arrived_ref = bf16[3,384,256]{2,1,0:T(8,128)(2,1)S(1)} collective-permute-done((bf16[3,384,256]{2,1,0:T(8,128)(2,1)}, bf16[3,384,256]{2,1,0:T(8,128)(2,1)S(1)}, u32[]{:S(2)}, u32[]{:S(2)}) %collective-permute-start.20) | collective-permute-done | bytes 589856 | tf_op jit(solution)/shard_map/ppermute | solution.py:26
  202.9 2.9 %add_block.4.refs_0_ = f32[3,384,1024]{2,1,0:T(8,128)} custom-call(s32[2]{0:T(128)} %pad_add_fusion.3.blocks_ref, f32[3,384,256]{2,1,0:T(8,128)} %kernel_sums.14.near_ref, bf16[3,384,256]{2,1,0:T(8,128)(2,1)} %copy-done.16), custom_call_target="tpu_custom_call" | custom-call | flops 294912 | bytes 2949120 | tf_op jit(solution)/shard_map/add_block/pallas_call | solution.py:143
  206.7 2.9 %add_block.5.refs_0_ = f32[3,384,1024]{2,1,0:T(8,128)} custom-call(s32[2]{0:T(128)} %pad_add_fusion.2.blocks_ref, f32[3,384,256]{2,1,0:T(8,128)} %kernel_sums.12.near_ref, bf16[3,384,256]{2,1,0:T(8,128)(2,1)} %copy-done.14, f32[3,384,1024]{2,1,0:T(8,128)} %add_block.4.refs_0_), custom_call_target="tpu_custom_call", output_to_operand_aliasing={{}: (3, {})} | custom-call | flops 294912 | bytes 2949120 | tf_op jit(solution)/shard_map/add_block/pallas_call | solution.py:143
  210.6 10.5 %kernel_sums.9 = bf16[3,384,256]{2,1,0:T(8,128)(2,1)} custom-call(s32[2]{0:T(128)} %pad_add_fusion.blocks_ref, bf16[3,128,3072]{2,1,0:T(8,128)(2,1)} %shifted_active.4.own_a, bf16[3,128,3072]{2,1,0:T(8,128)(2,1)} %shifted_active.5.pair_a, bf16[66,48,1024]{2,1,0:T(8,128)(2,1)} %copy-done, bf16[66,48,1024]{2,1,0:T(8,128)(2,1)} %copy-done, ...), custom_call_target="tpu_custom_call" | custom-call | flops 3623878656 | bytes 9043968 | tf_op jit(solution)/shard_map/kernel_sums/pallas_call | solution.py:112
  223.1 10.7 %kernel_sums.11 = bf16[3,384,256]{2,1,0:T(8,128)(2,1)} custom-call(s32[2]{0:T(128)} %pad_add_fusion.1.blocks_ref, bf16[3,128,3072]{2,1,0:T(8,128)(2,1)} %shifted_active.4.own_a, bf16[3,128,3072]{2,1,0:T(8,128)(2,1)} %shifted_active.5.pair_a, bf16[66,48,1024]{2,1,0:T(8,128)(2,1)} %copy-done, bf16[66,48,1024]{2,1,0:T(8,128)(2,1)} %copy-done, ...), custom_call_target="tpu_custom_call" | custom-call | flops 3623878656 | bytes 9043968 | tf_op jit(solution)/shard_map/kernel_sums/pallas_call | solution.py:112
  234.1 10.7 %kernel_sums.8.near_ref = f32[3,384,256]{2,1,0:T(8,128)} custom-call(s32[2]{0:T(128)} %pad_add_fusion.blocks_ref, bf16[3,128,6144]{2,1,0:T(8,128)(2,1)} %shifted_active.3.own_a.pair_a, bf16[3,128,6144]{2,1,0:T(8,128)(2,1)} %shifted_active.3.own_a.pair_a, bf16[66,48,1024]{2,1,0:T(8,128)(2,1)} %copy-done, bf16[66,48,1024]{2,1,0:T(8,128)(2,1)} %copy-done, ...), custom_call_target="tpu_custom_call" | custom-call | flops 3623878656 | bytes 9043968 | tf_op jit(solution)/shard_map/kernel_sums/pallas_call | solution.py:112
  244.8 10.7 %kernel_sums.10.near_ref = f32[3,384,256]{2,1,0:T(8,128)} custom-call(s32[2]{0:T(128)} %pad_add_fusion.1.blocks_ref, bf16[3,128,6144]{2,1,0:T(8,128)(2,1)} %shifted_active.3.own_a.pair_a, bf16[3,128,6144]{2,1,0:T(8,128)(2,1)} %shifted_active.3.own_a.pair_a, bf16[66,48,1024]{2,1,0:T(8,128)(2,1)} %copy-done, bf16[66,48,1024]{2,1,0:T(8,128)(2,1)} %copy-done, ...), custom_call_target="tpu_custom_call" | custom-call | flops 3623878656 | bytes 9043968 | tf_op jit(solution)/shard_map/kernel_sums/pallas_call | solution.py:112
  255.5 5.9 %collective-permute-done.16.arrived_ref = bf16[3,384,256]{2,1,0:T(8,128)(2,1)S(1)} collective-permute-done((bf16[3,384,256]{2,1,0:T(8,128)(2,1)}, bf16[3,384,256]{2,1,0:T(8,128)(2,1)S(1)}, u32[]{:S(2)}, u32[]{:S(2)}) %collective-permute-start.16) | collective-permute-done | bytes 589856 | tf_op jit(solution)/shard_map/ppermute | solution.py:26
  262.3 2.9 %add_block.6.refs_0_ = f32[3,384,1024]{2,1,0:T(8,128)} custom-call(s32[2]{0:T(128)} %pad_add_fusion.1.blocks_ref, f32[3,384,256]{2,1,0:T(8,128)} %kernel_sums.10.near_ref, bf16[3,384,256]{2,1,0:T(8,128)(2,1)} %copy-done.17, f32[3,384,1024]{2,1,0:T(8,128)} %add_block.5.refs_0_), custom_call_target="tpu_custom_call", output_to_operand_aliasing={{}: (3, {})} | custom-call | flops 294912 | bytes 2949120 | tf_op jit(solution)/shard_map/add_block/pallas_call | solution.py:143
  266.1 2.9 %add_block.7 = f32[3,384,1024]{2,1,0:T(8,128)} custom-call(s32[2]{0:T(128)} %pad_add_fusion.blocks_ref, f32[3,384,256]{2,1,0:T(8,128)} %kernel_sums.8.near_ref, bf16[3,384,256]{2,1,0:T(8,128)(2,1)} %copy-done.15, f32[3,384,1024]{2,1,0:T(8,128)} %add_block.6.refs_0_), custom_call_target="tpu_custom_call", output_to_operand_aliasing={{}: (3, {})} | custom-call | flops 294912 | bytes 2949120 | tf_op jit(solution)/shard_map/add_block/pallas_call | solution.py:143
  (84 shorter events, 23.0 us)
Async XLA Ops:
  2.2 12.2 %collective-permute-start = (bf16[1,48,1024]{2,1,0:T(8,128)(2,1)S(1)}, bf16[1,48,1024]{2,1,0:T(8,128)(2,1)S(1)}, u32[]{:S(2)}, u32[]{:S(2)}) collective-permute-start(bf16[1,48,1024]{2,1,0:T(8,128)(2,1)S(1)} %get-tuple-element.5), channel_id=1, source_target_pairs={{0,1},{1,2},{2,3},{4,5},{5,6},{6,7},{8,9},{9,10},{10,11},{12,13},{... | collective-permute-start | bytes 294920 | tf_op jit(solution)/shard_map/ppermute | solution.py:225
  5.4 13.1 %collective-permute-start.1 = (bf16[1,48,1024]{2,1,0:T(8,128)(2,1)}, bf16[1,48,1024]{2,1,0:T(8,128)(2,1)S(1)}, u32[]{:S(2)}, u32[]{:S(2)}) collective-permute-start(bf16[1,48,1024]{2,1,0:T(8,128)(2,1)} %get-tuple-element.4), channel_id=1, source_target_pairs={{1,0},{2,1},{3,2},{5,4},{6,5},{7,6},{9,8},{10,9},{11,10},{13,12},{... | collective-permute-start | bytes 294920 | tf_op jit(solution)/shard_map/ppermute | solution.py:226
  10.2 57.9 %collective-permute-start.4 = (bf16[64,24,128]{2,1,0:T(8,128)(2,1)}, bf16[64,24,128]{2,1,0:T(8,128)(2,1)}, u32[]{:S(2)}, u32[]{:S(2)}) collective-permute-start(bf16[64,24,128]{2,1,0:T(8,128)(2,1)} %get-tuple-element.7), channel_id=1, source_target_pairs={{0,1},{1,0},{2,3},{3,2},{4,5},{5,4},{6,7},{7,6},{8,9},{9,8},{10,11... | collective-permute-start | bytes 1179656 | tf_op jit(solution)/shard_map/ppermute | solution.py:26
  10.2 59.8 %collective-permute-start.9 = (bf16[64,24,128]{2,1,0:T(8,128)(2,1)}, bf16[64,24,128]{2,1,0:T(8,128)(2,1)}, u32[]{:S(2)}, u32[]{:S(2)}) collective-permute-start(bf16[64,24,128]{2,1,0:T(8,128)(2,1)} %get-tuple-element.9.refs_0_), channel_id=1, source_target_pairs={{0,16},{16,0},{1,17},{17,1},{2,18},{18,2},{3,19},{19,3},{4,20},{20... | collective-permute-start | bytes 1179656 | tf_op jit(solution)/shard_map/ppermute | solution.py:26
  11.5 59.8 %collective-permute-start.10 = (bf16[64,24,128]{2,1,0:T(8,128)(2,1)}, bf16[64,24,128]{2,1,0:T(8,128)(2,1)}, u32[]{:S(2)}, u32[]{:S(2)}) collective-permute-start(bf16[64,24,128]{2,1,0:T(8,128)(2,1)} %get-tuple-element.6), channel_id=1, source_target_pairs={{0,1},{1,0},{2,3},{3,2},{4,5},{5,4},{6,7},{7,6},{8,9},{9,8},{10,11... | collective-permute-start | bytes 1179656 | tf_op jit(solution)/shard_map/ppermute | solution.py:26
  18.5 2.7 %copy-start = (bf16[66,48,1024]{2,1,0:T(8,128)(2,1)}, bf16[66,48,1024]{2,1,0:T(8,128)(2,1)S(1)}, u32[]{:S(2)}) copy-start(bf16[66,48,1024]{2,1,0:T(8,128)(2,1)S(1)} %constant_dynamic-update-slice_fusion.grad_ref.refs_0_.refs_1_) | copy-start | bytes 19464196
  65.0 1.7 copy-start.11
  66.1 2.9 %copy-start.12 = (bf16[32,48,512]{2,1,0:T(8,128)(2,1)S(1)}, bf16[32,48,512]{2,1,0:T(8,128)(2,1)}, u32[]{:S(2)}) copy-start(bf16[32,48,512]{2,1,0:T(8,128)(2,1)} %block_grad.3) | copy-start | bytes 4718596
  66.1 44.4 %collective-permute-start.6 = (bf16[66,48,128]{2,1,0:T(8,128)(2,1)}, bf16[66,48,128]{2,1,0:T(8,128)(2,1)S(1)}, u32[]{:S(2)}, u32[]{:S(2)}) collective-permute-start(bf16[66,48,128]{2,1,0:T(8,128)(2,1)} %pad_maximum_fusion.1), channel_id=1, source_target_pairs={{0,1},{1,0},{2,3},{3,2},{4,5},{5,4},{6,7},{7,6},{8,9},{9,8},{10,11... | collective-permute-start | bytes 2433032 | tf_op jit(solution)/shard_map/ppermute | solution.py:26
  67.8 56.4 %collective-permute-start.2 = (bf16[32,24,512]{2,1,0:T(8,128)(2,1)}, bf16[32,24,512]{2,1,0:T(8,128)(2,1)}, u32[]{:S(2)}, u32[]{:S(2)}) collective-permute-start(bf16[32,24,512]{2,1,0:T(8,128)(2,1)} %constant_dynamic-slice_fusion.11), channel_id=1, source_target_pairs={{0,16},{16,0},{1,17},{17,1},{2,18},{18,2},{3,19},{19,3},{4,20},{20... | collective-permute-start | bytes 2359304 | tf_op jit(solution)/shard_map/ppermute | solution.py:26
  68.0 4.1 %copy-start.13 = (bf16[64,24,128]{2,1,0:T(8,128)(2,1)S(1)}, bf16[64,24,128]{2,1,0:T(8,128)(2,1)}, u32[]{:S(2)}) copy-start(bf16[64,24,128]{2,1,0:T(8,128)(2,1)} %get-tuple-element.8) | copy-start | bytes 1179652
  68.1 57.4 %collective-permute-start.13 = (bf16[66,48,128]{2,1,0:T(8,128)(2,1)S(1)}, bf16[66,48,128]{2,1,0:T(8,128)(2,1)S(1)}, u32[]{:S(2)}, u32[]{:S(2)}) collective-permute-start(bf16[66,48,128]{2,1,0:T(8,128)(2,1)S(1)} %pad_maximum_fusion.2), channel_id=1, source_target_pairs={{0,1},{1,0},{2,3},{3,2},{4,5},{5,4},{6,7},{7,6},{8,9},{9,8},{10,11... | collective-permute-start | bytes 2433032 | tf_op jit(solution)/shard_map/ppermute | solution.py:26
  70.0 55.9 %collective-permute-start.3 = (bf16[32,24,512]{2,1,0:T(8,128)(2,1)}, bf16[32,24,512]{2,1,0:T(8,128)(2,1)}, u32[]{:S(2)}, u32[]{:S(2)}) collective-permute-start(bf16[32,24,512]{2,1,0:T(8,128)(2,1)} %constant_dynamic-slice_fusion.10), channel_id=1, source_target_pairs={{0,16},{16,0},{1,17},{17,1},{2,18},{18,2},{3,19},{19,3},{4,20},{20... | collective-permute-start | bytes 2359304 | tf_op jit(solution)/shard_map/ppermute | solution.py:26
  71.2 39.0 %collective-permute-start.11 = (bf16[64,24,128]{2,1,0:T(8,128)(2,1)}, bf16[64,24,128]{2,1,0:T(8,128)(2,1)S(1)}, u32[]{:S(2)}, u32[]{:S(2)}) collective-permute-start(bf16[64,24,128]{2,1,0:T(8,128)(2,1)} %collective-permute-done.10.refs_0_), channel_id=1, source_target_pairs={{0,16},{16,0},{1,17},{17,1},{2,18},{18,2},{3,19},{19,3},{4,20},{20... | collective-permute-start | bytes 1179656 | tf_op jit(solution)/shard_map/ppermute | solution.py:26
  73.2 46.7 %copy-start.10 = (bf16[128,24,128]{2,1,0:T(8,128)(2,1)}, bf16[128,24,128]{2,1,0:T(8,128)(2,1)S(1)}, u32[]{:S(2)}) copy-start(bf16[128,24,128]{2,1,0:T(8,128)(2,1)S(1)} %pad_maximum_fusion.3.refs_0_) | copy-start | bytes 2359300
  110.2 5.4 %copy-start.18 = (bf16[64,24,128]{2,1,0:T(8,128)(2,1)}, bf16[64,24,128]{2,1,0:T(8,128)(2,1)S(1)}, u32[]{:S(2)}) copy-start(bf16[64,24,128]{2,1,0:T(8,128)(2,1)S(1)} %collective-permute-done.11.refs_1_) | copy-start | bytes 1179652
  110.2 19.9 %collective-permute-start.5 = (bf16[128,24,128]{2,1,0:T(8,128)(2,1)S(1)}, bf16[128,24,128]{2,1,0:T(8,128)(2,1)}, u32[]{:S(2)}, u32[]{:S(2)}) collective-permute-start(bf16[128,24,128]{2,1,0:T(8,128)(2,1)S(1)} %pad_maximum_fusion.3.refs_0_), channel_id=1, source_target_pairs={{0,16},{16,0},{1,17},{17,1},{2,18},{18,2},{3,19},{19,3},{4,20},{20... | collective-permute-start | bytes 2359304 | tf_op jit(solution)/shard_map/ppermute | solution.py:26
  110.5 13.7 %copy-start.2 = (bf16[66,48,128]{2,1,0:T(8,128)(2,1)}, bf16[66,48,128]{2,1,0:T(8,128)(2,1)S(1)}, u32[]{:S(2)}) copy-start(bf16[66,48,128]{2,1,0:T(8,128)(2,1)S(1)} %collective-permute-done.6.refs_2_) | copy-start | bytes 2433028
  110.5 26.9 %collective-permute-start.17 = (bf16[66,48,128]{2,1,0:T(8,128)(2,1)S(1)}, bf16[66,48,128]{2,1,0:T(8,128)(2,1)S(1)}, u32[]{:S(2)}, u32[]{:S(2)}) collective-permute-start(bf16[66,48,128]{2,1,0:T(8,128)(2,1)S(1)} %collective-permute-done.6.refs_2_), channel_id=1, source_target_pairs={{0,4},{4,0},{8,12},{12,8},{1,5},{5,1},{9,13},{13,9},{2,6},{6,2},{1... | collective-permute-start | bytes 2433032 | tf_op jit(solution)/shard_map/ppermute | solution.py:26
  119.9 6.0 %copy-start.1 = (bf16[64,24,512]{2,1,0:T(8,128)(2,1)S(1)}, bf16[64,24,512]{2,1,0:T(8,128)(2,1)}, u32[]{:S(2)}) copy-start(bf16[64,24,512]{2,1,0:T(8,128)(2,1)} %param.3) | copy-start | bytes 4718596
  124.2 26.6 %collective-permute-start.7 = (bf16[66,48,128]{2,1,0:T(8,128)(2,1)S(1)}, bf16[66,48,128]{2,1,0:T(8,128)(2,1)S(1)}, u32[]{:S(2)}, u32[]{:S(2)}) collective-permute-start(bf16[66,48,128]{2,1,0:T(8,128)(2,1)S(1)} %collective-permute-done.6.refs_2_), channel_id=1, source_target_pairs={{0,8},{4,12},{8,0},{12,4},{1,9},{5,13},{9,1},{13,5},{2,10},{6,14},... | collective-permute-start | bytes 2433032 | tf_op jit(solution)/shard_map/ppermute | solution.py:26
  125.5 3.0 %copy-start.3 = (bf16[66,48,128]{2,1,0:T(8,128)(2,1)}, bf16[66,48,128]{2,1,0:T(8,128)(2,1)S(1)}, u32[]{:S(2)}) copy-start(bf16[66,48,128]{2,1,0:T(8,128)(2,1)S(1)} %collective-permute-done.13.refs_2_) | copy-start | bytes 2433028
  125.5 26.1 %collective-permute-start.19 = (bf16[66,48,128]{2,1,0:T(8,128)(2,1)S(1)}, bf16[66,48,128]{2,1,0:T(8,128)(2,1)S(1)}, u32[]{:S(2)}, u32[]{:S(2)}) collective-permute-start(bf16[66,48,128]{2,1,0:T(8,128)(2,1)S(1)} %collective-permute-done.13.refs_2_), channel_id=1, source_target_pairs={{0,4},{4,0},{8,12},{12,8},{1,5},{5,1},{9,13},{13,9},{2,6},{6,2},{1... | collective-permute-start | bytes 2433032 | tf_op jit(solution)/shard_map/ppermute | solution.py:26
  128.5 34.5 %collective-permute-start.14 = (bf16[66,48,128]{2,1,0:T(8,128)(2,1)S(1)}, bf16[66,48,128]{2,1,0:T(8,128)(2,1)S(1)}, u32[]{:S(2)}, u32[]{:S(2)}) collective-permute-start(bf16[66,48,128]{2,1,0:T(8,128)(2,1)S(1)} %collective-permute-done.13.refs_2_), channel_id=1, source_target_pairs={{0,8},{4,12},{8,0},{12,4},{1,9},{5,13},{9,1},{13,5},{2,10},{6,14},... | collective-permute-start | bytes 2433032 | tf_op jit(solution)/shard_map/ppermute | solution.py:26
  148.7 57.1 %collective-permute-start.18 = (bf16[3,384,256]{2,1,0:T(8,128)(2,1)}, bf16[3,384,256]{2,1,0:T(8,128)(2,1)S(1)}, u32[]{:S(2)}, u32[]{:S(2)}) collective-permute-start(bf16[3,384,256]{2,1,0:T(8,128)(2,1)} %kernel_sums.13), channel_id=1, source_target_pairs={{0,3},{1,2},{2,1},{3,0},{4,7},{5,6},{6,5},{7,4},{8,11},{9,10},{10,... | collective-permute-start | bytes 1769480 | tf_op jit(solution)/shard_map/ppermute | solution.py:26
  150.8 12.2 %copy-start.4 = (bf16[66,48,128]{2,1,0:T(8,128)(2,1)}, bf16[66,48,128]{2,1,0:T(8,128)(2,1)S(1)}, u32[]{:S(2)}) copy-start(bf16[66,48,128]{2,1,0:T(8,128)(2,1)S(1)} %collective-permute-done.7.refs_2_) | copy-start | bytes 2433028
  150.8 58.9 %collective-permute-start.8 = (bf16[66,48,128]{2,1,0:T(8,128)(2,1)S(1)}, bf16[66,48,128]{2,1,0:T(8,128)(2,1)S(1)}, u32[]{:S(2)}, u32[]{:S(2)}) collective-permute-start(bf16[66,48,128]{2,1,0:T(8,128)(2,1)S(1)} %collective-permute-done.7.refs_2_), channel_id=1, source_target_pairs={{0,4},{4,0},{8,12},{12,8},{1,5},{5,1},{9,13},{13,9},{2,6},{6,2},{1... | collective-permute-start | bytes 2433032 | tf_op jit(solution)/shard_map/ppermute | solution.py:26
  163.0 39.1 %collective-permute-start.20 = (bf16[3,384,256]{2,1,0:T(8,128)(2,1)}, bf16[3,384,256]{2,1,0:T(8,128)(2,1)S(1)}, u32[]{:S(2)}, u32[]{:S(2)}) collective-permute-start(bf16[3,384,256]{2,1,0:T(8,128)(2,1)} %kernel_sums.15), channel_id=1, source_target_pairs={{0,3},{1,2},{2,1},{3,0},{4,7},{5,6},{6,5},{7,4},{8,11},{9,10},{10,... | collective-permute-start | bytes 1769480 | tf_op jit(solution)/shard_map/ppermute | solution.py:26
  163.0 10.9 %copy-start.6 = (bf16[66,48,128]{2,1,0:T(8,128)(2,1)}, bf16[66,48,128]{2,1,0:T(8,128)(2,1)S(1)}, u32[]{:S(2)}) copy-start(bf16[66,48,128]{2,1,0:T(8,128)(2,1)S(1)} %collective-permute-done.14.refs_2_) | copy-start | bytes 2433028
  163.1 59.1 %collective-permute-start.15 = (bf16[66,48,128]{2,1,0:T(8,128)(2,1)S(1)}, bf16[66,48,128]{2,1,0:T(8,128)(2,1)S(1)}, u32[]{:S(2)}, u32[]{:S(2)}) collective-permute-start(bf16[66,48,128]{2,1,0:T(8,128)(2,1)S(1)} %collective-permute-done.14.refs_2_), channel_id=1, source_target_pairs={{0,4},{4,0},{8,12},{12,8},{1,5},{5,1},{9,13},{13,9},{2,6},{6,2},{1... | collective-permute-start | bytes 2433032 | tf_op jit(solution)/shard_map/ppermute | solution.py:26
  221.0 44.2 %collective-permute-start.12 = (bf16[3,384,256]{2,1,0:T(8,128)(2,1)}, bf16[3,384,256]{2,1,0:T(8,128)(2,1)S(1)}, u32[]{:S(2)}, u32[]{:S(2)}) collective-permute-start(bf16[3,384,256]{2,1,0:T(8,128)(2,1)} %kernel_sums.9), channel_id=1, source_target_pairs={{0,3},{1,2},{2,1},{3,0},{4,7},{5,6},{6,5},{7,4},{8,11},{9,10},{10,... | collective-permute-start | bytes 1769480 | tf_op jit(solution)/shard_map/ppermute | solution.py:26
  233.8 27.7 %collective-permute-start.16 = (bf16[3,384,256]{2,1,0:T(8,128)(2,1)}, bf16[3,384,256]{2,1,0:T(8,128)(2,1)S(1)}, u32[]{:S(2)}, u32[]{:S(2)}) collective-permute-start(bf16[3,384,256]{2,1,0:T(8,128)(2,1)} %kernel_sums.11), channel_id=1, source_target_pairs={{0,3},{1,2},{2,1},{3,0},{4,7},{5,6},{6,5},{7,4},{8,11},{9,10},{10,... | collective-permute-start | bytes 1769480 | tf_op jit(solution)/shard_map/ppermute | solution.py:26
  (8 other events, 6.9 us)
